TPU v7x, 256 devices: a whole 4x4x8 slice. The times are simulated.
256 devices in a mesh: seq: 32 (over y, x, core), head: 8 (over z).
Axes of the slice: x: 4, y: 4, z: 8, core: 2. Of those that a mesh axis runs over, the one named last changes fastest.
Arguments:
- queries: bfloat16 [32768, 32, 128], P('seq', 'head'), may hold values from -6 to 6
- key_vectors: bfloat16 [32768, 32, 128], P('seq', 'head'), may hold values from -6 to 6
- value_vectors: bfloat16 [32768, 32, 128], P('seq', 'head'), may hold values from -6 to 6
- out_grad: bfloat16 [32768, 32, 128], P(('seq', 'head')), may hold values from -6 to 6
Outputs:
- attended: bfloat16 [32768, 32, 128], P(('seq', 'head'))
- query_grad: bfloat16 [32768, 32, 128], P('seq', 'head')
- key_grad: bfloat16 [32768, 32, 128], P('seq', 'head')
- value_grad: bfloat16 [32768, 32, 128], P('seq', 'head')
All inputs are finite; a program needn't handle non-finite values.
Results may differ from a plain program's by a relative error of at most 0.0058.
Values may be sent and summed in bfloat16 or wider, within the bound.
A program may use at most 128 MiB of HBM per device.

v0:
```python
import jax
import jax.numpy as jnp
from jax import lax
from jax.sharding import PartitionSpec as P


def per_device(queries, key_vectors, value_vectors, out_grad):
    tok_rows, heads_local, head_size = queries.shape
    grad_full = lax.all_to_all(out_grad, "head", split_axis=1, concat_axis=0, tiled=True)
    position = (lax.axis_index("seq") * tok_rows + lax.iota(jnp.int32, tok_rows)).astype(
        jnp.float32
    )
    scaling = 1.0 / jnp.sqrt(head_size * (position + 1.0))
    scaled_grad = (scaling[:, None, None] * grad_full.astype(jnp.float32)).astype(jnp.bfloat16)
    seg_state = jnp.einsum(
        "shd,she->hde", key_vectors, value_vectors, preferred_element_type=jnp.float32
    )
    grad_state = jnp.einsum(
        "thd,the->hde", queries, scaled_grad, preferred_element_type=jnp.float32
    )
    pieces = (
        lax.all_gather(seg_state[None], "seq", axis=0, tiled=True),
        lax.all_gather(grad_state[None], "seq", axis=0, tiled=True),
    )
    piece_rows = pieces[0].shape[0]
    index_rows = lax.iota(jnp.int32, piece_rows)
    own_index = lax.axis_index("seq")
    below_mask = (index_rows < own_index).astype(jnp.float32)[:, None, None, None]
    above_mask = (index_rows > own_index).astype(jnp.float32)[:, None, None, None]
    prefix_sum = jnp.sum(below_mask * pieces[0], axis=0)
    suffix_sum = jnp.sum(above_mask * pieces[1], axis=0)
    prefix = prefix_sum.astype(jnp.bfloat16)
    suffix = suffix_sum.astype(jnp.bfloat16)
    block_rows = min(512, tok_rows)
    attended_blocks = []
    query_blocks = []
    key_accum = jnp.zeros((tok_rows, heads_local, head_size), jnp.float32)
    value_accum = jnp.zeros((tok_rows, heads_local, head_size), jnp.float32)
    for block_index in range(tok_rows // block_rows):
        row_start = block_index * block_rows
        row_end = row_start + block_rows
        query_block = queries[row_start:row_end]
        grad_block = scaled_grad[row_start:row_end]
        key_past = key_vectors[:row_end]
        value_past = value_vectors[:row_end]
        causal = (
            lax.iota(jnp.int32, row_end)[None, :]
            <= (row_start + lax.iota(jnp.int32, block_rows))[:, None]
        )[None]
        within = jnp.where(
            causal,
            jnp.einsum("thd,shd->hts", query_block, key_past, preferred_element_type=jnp.float32),
            0.0,
        ).astype(jnp.bfloat16)
        grad_scores = jnp.where(
            causal,
            jnp.einsum("thd,shd->hts", grad_block, value_past, preferred_element_type=jnp.float32),
            0.0,
        ).astype(jnp.bfloat16)
        carried = jnp.einsum(
            "thd,hde->the", query_block, prefix, preferred_element_type=jnp.float32
        )
        local_sum = jnp.einsum(
            "hts,shd->thd", within, value_past, preferred_element_type=jnp.float32
        )
        attended_blocks.append(
            (scaling[row_start:row_end, None, None] * (carried + local_sum)).astype(jnp.bfloat16)
        )
        query_part = jnp.einsum(
            "the,hde->thd", grad_block, prefix, preferred_element_type=jnp.float32
        )
        query_part = query_part + jnp.einsum(
            "hts,shd->thd", grad_scores, key_past, preferred_element_type=jnp.float32
        )
        query_blocks.append(query_part.astype(jnp.bfloat16))
        key_accum = key_accum.at[:row_end].add(
            jnp.einsum("hts,thd->shd", grad_scores, query_block, preferred_element_type=jnp.float32)
        )
        value_accum = value_accum.at[:row_end].add(
            jnp.einsum("hts,the->she", within, grad_block, preferred_element_type=jnp.float32)
        )
    key_grad = key_accum + jnp.einsum(
        "shj,hij->shi", value_vectors, suffix, preferred_element_type=jnp.float32
    )
    value_grad = value_accum + jnp.einsum(
        "shi,hij->shj", key_vectors, suffix, preferred_element_type=jnp.float32
    )
    attended_heads = jnp.concatenate(attended_blocks, axis=0)
    attended = lax.all_to_all(attended_heads, "head", split_axis=0, concat_axis=1, tiled=True)
    query_grad = jnp.concatenate(query_blocks, axis=0)
    return (attended, query_grad, key_grad.astype(jnp.bfloat16), value_grad.astype(jnp.bfloat16))


def solution(mesh):
    return jax.shard_map(
        per_device,
        mesh=mesh,
        in_specs=(
            P("seq", "head", None),
            P("seq", "head", None),
            P("seq", "head", None),
            P(("seq", "head"), None, None),
        ),
        out_specs=(
            P(("seq", "head"), None, None),
            P("seq", "head", None),
            P("seq", "head", None),
            P("seq", "head", None),
        ),
        check_vma=False,
    )
```

profile of v0, /device:TPU:1, one launch (start us, length us, event | category | flops | bytes accessed | tf_op | source)
XLA Modules:
  0.0 153.7 jit_solution(15245466234268388935)
XLA Ops:
  7.2 0.0 all-gather.5.cloned.1.call-start
  7.2 2.9 %fusion.34 = f32[4,128,128]{2,1,0:T(8,128)} fusion(bf16[1024,4,128]{2,1,0:T(4,128)(2,1)} %param.17, bf16[1024,4,128]{2,1,0:T(4,128)(2,1)} %param.18), kind=kOutput, calls=%fused_computation.64 | convolution fusion | flops 134217728 | bytes 2359296 | tf_op jit(solution)/shard_map/shd,she->hde/dot_general | solution.py:15
  10.1 1.4 copy.87
  11.5 9.0 %all-to-all-start.1 = ((bf16[128,32,128]{2,0,1:T(8,128)(2,1)}), bf16[128,32,128]{2,0,1:T(8,128)(2,1)S(1)}, u32[]{:S(2)}, u32[]{:S(2)}) async-start(bf16[128,32,128]{2,0,1:T(8,128)(2,1)} %copy.87), calls=%async_computation.1 | async-start | bytes 2097152 | tf_op jit(solution)/shard_map/all_to_all | solution.py:9
  20.6 29.1 %all-to-all-done.1 = bf16[128,32,128]{2,0,1:T(8,128)(2,1)S(1)} async-done(((bf16[128,32,128]{2,0,1:T(8,128)(2,1)}), bf16[128,32,128]{2,0,1:T(8,128)(2,1)S(1)}, u32[]{:S(2)}, u32[]{:S(2)}) %all-to-all-start.1) | async-done | bytes 1048608 | tf_op jit(solution)/shard_map/all_to_all | solution.py:9
  49.7 0.2 copy.88
  50.0 0.2 fusion
  50.2 1.0 copy-done.10
  51.2 0.5 convolution_bitcast_fusion.10
  51.7 0.9 copy.97
  52.6 0.1 copy.75
  52.8 0.1 copy.77
  52.9 1.2 copy-done.13
  54.1 0.1 copy.74
  54.3 0.1 iota_compare_fusion.1
  54.4 0.4 iota_compare_fusion
  54.8 0.7 select_convert_fusion.3
  55.5 1.8 %convolution_bitcast_fusion.3 = f32[512,4,128]{0,2,1:T(8,128)} fusion(bf16[4,512,512]{2,1,0:T(8,128)(2,1)S(1)} %select_convert_fusion.3, bf16[1024,4,128]{2,0,1:T(8,128)(2,1)S(1)} %copy.74), kind=kOutput, calls=%fused_computation.18 | convolution fusion | flops 268435456 | bytes 3670016 | tf_op jit(solution)/shard_map/hts,shd->thd/dot_general | solution.py:63
  57.3 1.4 select_convert_fusion.1
  58.8 0.7 select_convert_fusion.2
  59.5 1.9 %convolution_bitcast_fusion.1 = f32[512,4,128]{2,0,1:T(8,128)} fusion(bf16[4,512,512]{2,1,0:T(8,128)(2,1)S(1)} %select_convert_fusion.2, bf16[1024,4,128]{2,0,1:T(8,128)(2,1)S(1)} %copy.75), kind=kOutput, calls=%fused_computation.16 | convolution fusion | flops 268435456 | bytes 3670016 | tf_op jit(solution)/shard_map/hts,thd->shd/dot_general | solution.py:77
  61.4 1.8 %convolution_bitcast_fusion.2 = f32[512,4,128]{0,2,1:T(8,128)} fusion(bf16[4,512,512]{2,1,0:T(8,128)(2,1)S(1)} %select_convert_fusion.2, bf16[1024,4,128]{2,0,1:T(8,128)(2,1)S(1)} %copy.77), kind=kOutput, calls=%fused_computation.17 | convolution fusion | flops 268435456 | bytes 3670016 | tf_op jit(solution)/shard_map/hts,shd->thd/dot_general | solution.py:72
  63.2 1.5 convolution_bitcast_fusion
  64.7 1.4 select_convert_fusion
  66.2 3.1 %fusion.24 = f32[4,1024,128]{2,1,0:T(8,128)} fusion(bf16[4,512,1024]{2,1,0:T(8,128)(2,1)S(1)} %select_convert_fusion, bf16[1024,4,128]{2,0,1:T(8,128)(2,1)S(1)} %copy.75), kind=kOutput, calls=%fused_computation.50 | convolution fusion | flops 536870912 | bytes 6815744 | tf_op jit(solution)/shard_map/hts,thd->shd/dot_general | solution.py:77
  69.2 0.8 fusion.17
  70.0 3.3 %all-gather.5.cloned.1.call-done = f32[128,128,128]{2,1,0:T(8,128)} async-done(((f32[4,128,128]{2,1,0:T(8,128)}), f32[128,128,128]{2,1,0:T(8,128)}) %all-gather.5.cloned.1.call-update) | async-done | bytes 8388624 | tf_op jit(solution)/shard_map/all_gather | solution.py:22
  73.3 4.4 %multiply_reduce_fusion.1 = bf16[4,128,128]{2,1,0:T(8,128)(2,1)S(1)} fusion(f32[32,4,128,128]{3,2,1,0:T(8,128)} %bitcast.87, f32[32]{0:T(128)S(1)} %compare_convert_fusion.1), kind=kLoop, calls=%fused_computation.3 | loop fusion | flops 4128768 | bytes 8519808 | tf_op jit(solution)/shard_map/reduce_sum | solution.py:30
  77.8 0.4 convolution_bitcast_fusion.8
  78.1 0.8 copy-done.9
  79.0 0.5 fusion.9
  79.5 1.6 %fusion.10 = bf16[512,4,128]{0,2,1:T(8,128)(2,1)S(1)} fusion(f32[512,4,128]{0,2,1:T(8,128)S(1)} %convolution_bitcast_fusion.8, bf16[4,512,1024]{2,1,0:T(8,128)(2,1)S(1)} %copy-done.2, f32[512]{0:T(512)S(1)} %get-tuple-element.81, bf16[1024,4,128]{2,1,0:T(4,128)(2,1)S(1)} %copy-done.14), kind=kOutput, calls=%fused_computation.32 | convolution fusion | flops 537657344 | bytes 6817792 | tf_op jit(solution)/shard_map/hts,shd->thd/dot_general | solution.py:63
  81.1 1.1 pad_maximum_fusion
  82.2 2.4 %copy.85 = bf16[1024,4,128]{2,1,0:T(4,128)(2,1)} copy(bf16[1024,4,128]{0,2,1:T(8,128)(2,1)} %pad_maximum_fusion) | data formatting | bytes 2097152 | tf_op jit(solution)/shard_map/concatenate | solution.py:88
  84.6 6.7 %all-to-all-start = ((bf16[1024,4,128]{2,1,0:T(4,128)(2,1)}), bf16[1024,4,128]{2,1,0:T(4,128)(2,1)}, u32[]{:S(2)}, u32[]{:S(2)}) async-start(bf16[1024,4,128]{2,1,0:T(4,128)(2,1)} %copy.85), calls=%async_computation | async-start | bytes 2097152 | tf_op jit(solution)/shard_map/all_to_all | solution.py:89
  91.3 1.6 %fusion.11 = bf16[512,4,128]{0,2,1:T(8,128)(2,1)S(1)} fusion(f32[512,4,128]{0,2,1:T(8,128)} %convolution_bitcast_fusion.2, bf16[4,128,128]{2,1,0:T(8,128)(2,1)S(1)} %multiply_reduce_fusion.1, bf16[1024,4,128]{2,0,1:T(8,128)(2,1)S(1)} %fusion), kind=kOutput, calls=%fused_computation.33 | convolution fusion | flops 67633152 | bytes 2228224 | tf_op jit(solution)/shard_map/the,hde->thd/dot_general | solution.py:69
  93.0 0.3 convolution_bitcast_fusion.5
  93.3 3.9 %fusion.12 = bf16[512,4,128]{0,2,1:T(8,128)(2,1)S(1)} fusion(f32[512,4,128]{0,2,1:T(8,128)S(1)} %convolution_bitcast_fusion.5, bf16[4,512,1024]{2,1,0:T(8,128)(2,1)} %copy-done, bf16[1024,4,128]{2,1,0:T(4,128)(2,1)S(1)} %copy-done.6), kind=kOutput, calls=%fused_computation.34 | convolution fusion | flops 537395200 | bytes 6815744 | tf_op jit(solution)/shard_map/hts,shd->thd/dot_general | solution.py:72
  97.1 0.1 pad_maximum_fusion.1
  97.3 1.4 copy.104
  98.7 34.7 %all-gather.7.cloned.1.call-done = f32[128,128,128]{2,1,0:T(8,128)} async-done(((f32[4,128,128]{2,1,0:T(8,128)}), f32[128,128,128]{2,1,0:T(8,128)}) %all-gather.7.cloned.1.call-update) | async-done | bytes 8388624 | tf_op jit(solution)/shard_map/all_gather | solution.py:23
  133.5 4.4 %multiply_reduce_fusion = bf16[4,128,128]{2,1,0:T(8,128)(2,1)S(1)} fusion(f32[32,4,128,128]{3,2,1,0:T(8,128)} %bitcast.88, f32[32]{0:T(128)S(1)} %compare_convert_fusion), kind=kLoop, calls=%fused_computation | loop fusion | flops 4128768 | bytes 8519808 | tf_op jit(solution)/shard_map/reduce_sum | solution.py:31
  137.9 0.1 copy-done.15
  138.0 0.5 fusion.2
  138.5 1.8 %copy.105 = bf16[1024,4,128]{2,1,0:T(4,128)(2,1)} copy(bf16[1024,4,128]{2,0,1:T(8,128)(2,1)S(1)} %fusion.2) | data formatting | bytes 2097152
  140.3 1.6 %fusion.1 = bf16[1024,4,128]{0,2,1:T(8,128)(2,1)} fusion(f32[4,128,1024]{2,1,0:T(8,128)S(1)} %fusion.17, f32[512,4,128]{0,2,1:T(8,128)S(1)} %copy-done.11, bf16[4,128,128]{2,1,0:T(8,128)(2,1)S(1)} %multiply_reduce_fusion, bf16[1024,4,128]{2,1,0:T(4,128)(2,1)S(1)} %copy-done.7), kind=kOutput, calls=%fused_computation.9 | convolution fusion | flops 135790592 | bytes 5373952 | tf_op jit(solution)/shard_map/shi,hij->shj/dot_general | solution.py:85
  141.9 2.4 %copy.106 = bf16[1024,4,128]{2,1,0:T(4,128)(2,1)} copy(bf16[1024,4,128]{0,2,1:T(8,128)(2,1)} %fusion.1) | data formatting | bytes 2097152
  144.3 2.6 %copy.86 = bf16[128,8,4,128]{3,2,1,0:T(4,128)(2,1)} copy(bf16[128,8,4,128]{3,2,0,1:T(4,128)(2,1)} %bitcast.6) | data formatting | bytes 2097152 | tf_op jit(solution)/shard_map/all_to_all | solution.py:89
  (39 shorter events, 0.2 us)
Async XLA Ops:
  7.2 2.9 %copy-start.16 = (bf16[128,32,128]{2,1,0:T(8,128)(2,1)S(1)}, bf16[128,32,128]{2,1,0:T(8,128)(2,1)}, u32[]{:S(2)}) copy-start(bf16[128,32,128]{2,1,0:T(8,128)(2,1)} %param.19) | copy-start | bytes 3145732
  7.2 66.1 %all-gather.5.cloned.1.call-start = ((), (), s32[]{:S(2)}) async-start(), calls=%async_computation.2 | async-start | bytes 8650752 | tf_op jit(solution)/shard_map/all_gather | solution.py:22
  11.5 38.2 %all-to-all-start.1 = ((bf16[128,32,128]{2,0,1:T(8,128)(2,1)}), bf16[128,32,128]{2,0,1:T(8,128)(2,1)S(1)}, u32[]{:S(2)}, u32[]{:S(2)}) async-start(bf16[128,32,128]{2,0,1:T(8,128)(2,1)} %copy.87), calls=%async_computation.1 | async-start | bytes 2097152 | tf_op jit(solution)/shard_map/all_to_all | solution.py:9
  20.5 112.9 %all-gather.7.cloned.1.call-start = ((), (), s32[]{:S(2)}) async-start(), calls=%async_computation.3 | async-start | bytes 8650752 | tf_op jit(solution)/shard_map/all_gather | solution.py:23
  49.9 1.2 copy-start.10
  51.2 1.6 %copy-start.5 = (bf16[1024,4,128]{2,1,0:T(4,128)(2,1)S(1)}, bf16[1024,4,128]{2,1,0:T(4,128)(2,1)}, u32[]{:S(2)}) copy-start(bf16[1024,4,128]{2,1,0:T(4,128)(2,1)} %param.17) | copy-start | bytes 3145732
  52.6 1.6 %copy-start.13 = (bf16[1024,4,128]{2,1,0:T(4,128)(2,1)S(1)}, bf16[1024,4,128]{2,1,0:T(4,128)(2,1)}, u32[]{:S(2)}) copy-start(bf16[1024,4,128]{2,1,0:T(4,128)(2,1)} %param.18) | copy-start | bytes 3145732
  52.7 13.4 %copy-start.3 = (bf16[1024,4,128]{2,0,1:T(8,128)(2,1)}, bf16[1024,4,128]{2,0,1:T(8,128)(2,1)S(1)}, u32[]{:S(2)}) copy-start(bf16[1024,4,128]{2,0,1:T(8,128)(2,1)S(1)} %copy.75) | copy-start | bytes 3145732
  58.7 10.5 %copy-start.1 = (bf16[4,512,1024]{2,1,0:T(8,128)(2,1)}, bf16[4,512,1024]{2,1,0:T(8,128)(2,1)S(1)}, u32[]{:S(2)}) copy-start(bf16[4,512,1024]{2,1,0:T(8,128)(2,1)S(1)} %select_convert_fusion.1) | copy-start | bytes 12582916
  66.2 3.1 %copy-start = (bf16[4,512,1024]{2,1,0:T(8,128)(2,1)}, bf16[4,512,1024]{2,1,0:T(8,128)(2,1)S(1)}, u32[]{:S(2)}) copy-start(bf16[4,512,1024]{2,1,0:T(8,128)(2,1)S(1)} %select_convert_fusion) | copy-start | bytes 12582916
  73.3 4.4 %copy-start.4 = (bf16[1024,4,128]{2,0,1:T(8,128)(2,1)S(1)}, bf16[1024,4,128]{2,0,1:T(8,128)(2,1)}, u32[]{:S(2)}) copy-start(bf16[1024,4,128]{2,0,1:T(8,128)(2,1)} %copy-done.3) | copy-start | bytes 3145732
  73.3 6.2 %copy-start.2 = (bf16[4,512,1024]{2,1,0:T(8,128)(2,1)S(1)}, bf16[4,512,1024]{2,1,0:T(8,128)(2,1)}, u32[]{:S(2)}) copy-start(bf16[4,512,1024]{2,1,0:T(8,128)(2,1)} %copy-done.1) | copy-start | bytes 12582916
  77.7 1.2 copy-start.9
  77.8 1.8 %copy-start.14 = (bf16[1024,4,128]{2,1,0:T(4,128)(2,1)S(1)}, bf16[1024,4,128]{2,1,0:T(4,128)(2,1)}, u32[]{:S(2)}) copy-start(bf16[1024,4,128]{2,1,0:T(4,128)(2,1)} %param.18) | copy-start | bytes 3145732
  84.6 59.6 %all-to-all-start = ((bf16[1024,4,128]{2,1,0:T(4,128)(2,1)}), bf16[1024,4,128]{2,1,0:T(4,128)(2,1)}, u32[]{:S(2)}, u32[]{:S(2)}) async-start(bf16[1024,4,128]{2,1,0:T(4,128)(2,1)} %copy.85), calls=%async_computation | async-start | bytes 2097152 | tf_op jit(solution)/shard_map/all_to_all | solution.py:89
  91.3 1.9 %copy-start.6 = (bf16[1024,4,128]{2,1,0:T(4,128)(2,1)S(1)}, bf16[1024,4,128]{2,1,0:T(4,128)(2,1)}, u32[]{:S(2)}) copy-start(bf16[1024,4,128]{2,1,0:T(4,128)(2,1)} %param.17) | copy-start | bytes 3145732
  133.5 4.4 %copy-start.8 = (f32[4,1024,128]{2,1,0:T(8,128)S(1)}, f32[4,1024,128]{2,1,0:T(8,128)}, u32[]{:S(2)}) copy-start(f32[4,1024,128]{2,1,0:T(8,128)} %fusion.24) | copy-start | bytes 6291460
  133.5 4.4 %copy-start.12 = (f32[512,4,128]{2,0,1:T(8,128)S(1)}, f32[512,4,128]{2,0,1:T(8,128)}, u32[]{:S(2)}) copy-start(f32[512,4,128]{2,0,1:T(8,128)} %convolution_bitcast_fusion.1) | copy-start | bytes 3145732
  133.5 4.6 %copy-start.15 = (bf16[1024,4,128]{2,1,0:T(4,128)(2,1)S(1)}, bf16[1024,4,128]{2,1,0:T(4,128)(2,1)}, u32[]{:S(2)}) copy-start(bf16[1024,4,128]{2,1,0:T(4,128)(2,1)} %param.18) | copy-start | bytes 3145732
  138.5 1.8 %copy-start.7 = (bf16[1024,4,128]{2,1,0:T(4,128)(2,1)S(1)}, bf16[1024,4,128]{2,1,0:T(4,128)(2,1)}, u32[]{:S(2)}) copy-start(bf16[1024,4,128]{2,1,0:T(4,128)(2,1)} %param.17) | copy-start | bytes 3145732
  138.5 1.8 %copy-start.11 = (f32[512,4,128]{0,2,1:T(8,128)S(1)}, f32[512,4,128]{0,2,1:T(8,128)}, u32[]{:S(2)}) copy-start(f32[512,4,128]{0,2,1:T(8,128)} %convolution_bitcast_fusion) | copy-start | bytes 3145732
Sparse Core Ops, SparseCore 0:
  11.1 62.1 all-gather.4
  75.9 57.5 all-gather.6
where the time goes:
time: 154 us
  waiting for transfers between devices  67.2 us (44%)
  matrix products  28.8 us (19%)
  local copies, waits for them, and re-layouts  16.7 us (11%)
  starting transfers between devices  15.8 us (10%)
  between operations  14.4 us (9%)
  other arithmetic  10.8 us (7%)
    all_gather x1, waiting for transfers between devices, per_device(): lax.all_gather(grad_state[None], 'seq', axis=0, tiled=True)  34.7 us
    all_to_all x1, waiting for transfers between devices, per_device(): lax.all_to_all(out_grad, 'head', split_axis=1, concat_axis=0, tiled=True)  29.1 us
    unnamed x41, local copies, waits for them, and re-layouts  10.6 us
    all_to_all x1, starting transfers between devices, per_device(): lax.all_to_all(out_grad, 'head', split_axis=1, concat_axis=0, tiled=True)  9.01 us
    all_to_all x1, starting transfers between devices, per_device(): lax.all_to_all(attended_heads, 'head', split_axis=0, concat_axis=1, tiled...  6.72 us
    dot_general x2, matrix products, per_device(): jnp.einsum('hts,shd->thd', grad_scores, key_past, preferred_element_type=...  5.66 us
    dot_general x2, matrix products, per_device(): jnp.einsum('hts,thd->shd', grad_scores, query_block, preferred_element_ty...  4.95 us
    reduce_sum x1, other arithmetic, per_device(): prefix_sum = jnp.sum(below_mask * pieces[0], axis=0)  4.41 us
  transfers between devices with their start and end apart: 4, of which 3 were waited for; matrix products, arithmetic and copies ran while one was open for 31% of the time, Pallas kernels for 0%

commit v1 on v0

v1 whole, which is shorter than its diff:
```python
import jax
import jax.numpy as jnp
from jax import lax
from jax.experimental import pallas as pl
from jax.experimental.pallas import tpu as pltpu
from jax.sharding import PartitionSpec as P

MESH = pl.DeviceIdType.MESH
BF = jnp.bfloat16
F32 = jnp.float32

NSEQ = 32
NHEAD = 8
TOK = 1024
HL = 4
D = 128
ROWS = TOK * HL
BLK = TOK // NHEAD
CH = 256
NCH = ROWS // CH
PIECE = HL * D // NSEQ
SEND_ORDER = (4, 3, 5, 2, 6, 1, 7)


def nn(a, b):
    return lax.dot_general(a, b, (((1,), (0,)), ((), ())), preferred_element_type=F32)


def nt(a, b):
    return lax.dot_general(a, b, (((1,), (1,)), ((), ())), preferred_element_type=F32)


def tn(a, b):
    return lax.dot_general(a, b, (((0,), (0,)), ((), ())), preferred_element_type=F32)


def kernel(
    q_hbm, k_hbm, v_hbm, g_hbm,
    att_hbm, qg_hbm, kg_hbm, vg_hbm,
    q_buf, k_buf, v_buf, g_land, gs_buf, att_buf,
    att_loc, kg_loc, vg_loc, qg_buf, kg_buf, vg_buf,
    k_run, g_run, p_chunk, within_t, scale_buf,
    head_mask, tri_mask, tri_mask_t,
    acc, state_buf, piece_in, piece_out, prefix_buf,
    gstate_buf, gpiece_in, gpiece_out, suffix_buf,
    load_sem, out_sem, z_send, z_recv, own_sem, scan_send, scan_recv,
):
    me = lax.axis_index("seq")
    z = lax.axis_index("head")

    loads = []
    for i, (src, dst) in enumerate(((k_hbm, k_buf), (v_hbm, v_buf), (q_hbm, q_buf))):
        copy = pltpu.make_async_copy(src, dst, load_sem.at[i])
        copy.start()
        loads.append(copy)

    barrier = pltpu.get_barrier_semaphore()
    for d in range(1, NHEAD):
        pl.semaphore_signal(
            barrier, inc=1, device_id={"head": lax.rem(z + d, NHEAD)}, device_id_type=MESH
        )

    def greet(d, carry):
        pl.semaphore_signal(
            barrier, inc=1, device_id={"seq": lax.rem(me + d, NSEQ)}, device_id_type=MESH
        )
        return carry

    lax.fori_loop(1, NSEQ, greet, 0)
    pl.semaphore_wait(barrier, NHEAD - 1 + NSEQ - 1)

    grad_in = []
    for d in SEND_ORDER:
        to = lax.rem(z + d, NHEAD)
        copy = pltpu.make_async_remote_copy(
            src_ref=g_hbm.at[:, to],
            dst_ref=g_land.at[pl.ds(z * BLK, BLK)],
            send_sem=z_send.at[d],
            recv_sem=z_recv.at[d],
            device_id={"head": to},
            device_id_type=MESH,
        )
        copy.start()
        grad_in.append(copy)
    own_grad = pltpu.make_async_copy(g_hbm.at[:, z], g_land.at[pl.ds(z * BLK, BLK)], own_sem.at[0])
    own_grad.start()

    row = lax.broadcasted_iota(jnp.int32, (CH, HL * D), 0)
    col = lax.broadcasted_iota(jnp.int32, (CH, HL * D), 1)
    head_mask[...] = ((row & 3) == (col >> 7)).astype(F32).astype(BF)
    row = lax.broadcasted_iota(jnp.int32, (CH, CH), 0)
    col = lax.broadcasted_iota(jnp.int32, (CH, CH), 1)
    same = (row & 3) == (col & 3)
    tri_mask[...] = (same & (col <= row)).astype(F32).astype(BF)
    tri_mask_t[...] = (same & (row <= col)).astype(F32).astype(BF)

    def rows(c):
        return pl.ds(pl.multiple_of(c * CH, CH), CH)

    def spread(x):
        return jnp.concatenate([x] * HL, axis=1) * head_mask[...]

    def wide(stacked):
        return jnp.concatenate([stacked[h * D : (h + 1) * D] for h in range(HL)], axis=1)

    def stack(w):
        return jnp.concatenate([w[:, h * D : (h + 1) * D] for h in range(HL)], axis=0)

    def each_chunk(body):
        lax.fori_loop(0, NCH, lambda c, carry: (body(c), carry)[1], 0)

    def scatter_pieces(src, dst, k):
        def one(d, carry):
            to = lax.rem(me + d, NSEQ)
            pltpu.make_async_remote_copy(
                src_ref=src.at[pl.ds(pl.multiple_of(to * PIECE, PIECE), PIECE)],
                dst_ref=dst.at[me],
                send_sem=scan_send.at[k],
                recv_sem=scan_recv.at[k],
                device_id={"seq": to},
                device_id_type=MESH,
            ).start()
            return carry

        lax.fori_loop(1, NSEQ, one, 0)
        dst[me] = src[pl.ds(pl.multiple_of(me * PIECE, PIECE), PIECE)]

    def return_pieces(src, dst, k):
        def one(d, carry):
            to = lax.rem(me + d, NSEQ)
            pltpu.make_async_remote_copy(
                src_ref=src.at[to],
                dst_ref=dst.at[pl.ds(pl.multiple_of(me * PIECE, PIECE), PIECE)],
                send_sem=scan_send.at[k],
                recv_sem=scan_recv.at[k],
                device_id={"seq": to},
                device_id_type=MESH,
            ).start()
            return carry

        lax.fori_loop(1, NSEQ, one, 0)
        dst[pl.ds(pl.multiple_of(me * PIECE, PIECE), PIECE)] = src[me]

    def wait_pieces(ref, sem):
        part = ref.at[pl.ds(0, NSEQ - 1)]
        pltpu.make_async_copy(part, part, sem).wait()

    def wait_rows(ref, sem):
        part = ref.at[pl.ds(0, (NSEQ - 1) * PIECE)]
        pltpu.make_async_copy(part, part, sem).wait()

    acc[...] = jnp.zeros_like(acc)
    loads[0].wait()
    loads[1].wait()

    def key_state(c):
        k_run[c] = acc[...]
        acc[...] += tn(k_buf[rows(c)], spread(v_buf[rows(c)]))

    each_chunk(key_state)
    state_buf[...] = stack(acc[...])
    scatter_pieces(state_buf, piece_in, 0)

    loads[2].wait()

    def local_attend(c):
        q, k = q_buf[rows(c)], k_buf[rows(c)]
        within = nt(q, k).astype(BF) * tri_mask[...]
        att_loc[rows(c)] = nn(within, v_buf[rows(c)])
        token = lax.broadcasted_iota(jnp.int32, (CH, D), 0) >> 2
        position = (me * TOK + c * (CH // HL) + token).astype(F32)
        scale_buf[rows(c)] = 1.0 / jnp.sqrt(D * (position + 1.0))

    each_chunk(local_attend)

    wait_pieces(piece_in, scan_recv.at[0])

    def scan_up(j, run):
        piece_out[j] = run.astype(BF)
        return run + piece_in[j]

    lax.fori_loop(0, NSEQ, scan_up, jnp.zeros((PIECE, D), F32))
    return_pieces(piece_out, prefix_buf, 1)

    def local_within_t(c):
        within_t[c] = nt(k_buf[rows(c)], q_buf[rows(c)]).astype(BF) * tri_mask_t[...]

    each_chunk(local_within_t)
    wait_rows(prefix_buf, scan_recv.at[1])

    att_rows = att_buf.reshape(ROWS, D)

    def attend(c):
        prefix = (prefix_buf[...].astype(F32) + stack(k_run[c])).astype(BF)
        p_chunk[c] = prefix
        total = att_loc[rows(c)] + nn(spread(q_buf[rows(c)]), prefix)
        att_rows[rows(c)] = (scale_buf[rows(c)] * total).astype(BF)

    each_chunk(attend)

    own_grad.wait()
    for copy in grad_in:
        copy.wait_recv()

    att_out = []
    for d in SEND_ORDER:
        to = lax.rem(z + d, NHEAD)
        copy = pltpu.make_async_remote_copy(
            src_ref=att_buf.at[pl.ds(to * BLK, BLK)],
            dst_ref=att_hbm.at[:, z],
            send_sem=z_send.at[NHEAD + d],
            recv_sem=z_recv.at[NHEAD + d],
            device_id={"head": to},
            device_id_type=MESH,
        )
        copy.start()
        att_out.append(copy)
    own_att = pltpu.make_async_copy(
        att_buf.at[pl.ds(z * BLK, BLK)], att_hbm.at[:, z], own_sem.at[1]
    )
    own_att.start()

    g_rows = g_land.reshape(ROWS, D)
    acc[...] = jnp.zeros_like(acc)

    def grad_state(i):
        c = NCH - 1 - i
        g = (scale_buf[rows(c)] * g_rows[rows(c)].astype(F32)).astype(BF)
        gs_buf[rows(c)] = g
        g_run[c] = acc[...]
        acc[...] += tn(q_buf[rows(c)], spread(g))

    each_chunk(grad_state)
    gstate_buf[...] = stack(acc[...])
    scatter_pieces(gstate_buf, gpiece_in, 2)

    def query_grad(c):
        g = gs_buf[rows(c)]
        scores = nt(g, v_buf[rows(c)]).astype(BF) * tri_mask[...]
        total = nt(spread(g), wide(p_chunk[c])) + nn(scores, k_buf[rows(c)])
        qg_buf[rows(c)] = total.astype(BF)

    each_chunk(query_grad)
    qg_out = pltpu.make_async_copy(qg_buf, qg_hbm, out_sem.at[0])
    qg_out.start()

    wait_pieces(gpiece_in, scan_recv.at[2])

    def scan_down(i, run):
        j = NSEQ - 1 - i
        gpiece_out[j] = run.astype(BF)
        return run + gpiece_in[j]

    lax.fori_loop(0, NSEQ, scan_down, jnp.zeros((PIECE, D), F32))
    return_pieces(gpiece_out, suffix_buf, 3)

    def local_key_value(c):
        g = gs_buf[rows(c)]
        scores_t = nt(v_buf[rows(c)], g).astype(BF) * tri_mask_t[...]
        kg_loc[rows(c)] = nn(scores_t, q_buf[rows(c)])
        vg_loc[rows(c)] = nn(within_t[c], g)

    each_chunk(local_key_value)
    wait_rows(suffix_buf, scan_recv.at[3])

    def key_value(c):
        suffix = (suffix_buf[...].astype(F32) + stack(g_run[c])).astype(BF)
        kg = kg_loc[rows(c)] + nt(spread(v_buf[rows(c)]), wide(suffix))
        kg_buf[rows(c)] = kg.astype(BF)
        vg = vg_loc[rows(c)] + nn(spread(k_buf[rows(c)]), suffix)
        vg_buf[rows(c)] = vg.astype(BF)

    each_chunk(key_value)
    kg_out = pltpu.make_async_copy(kg_buf, kg_hbm, out_sem.at[1])
    kg_out.start()
    vg_out = pltpu.make_async_copy(vg_buf, vg_hbm, out_sem.at[2])
    vg_out.start()

    wait_rows(state_buf, scan_send.at[0])
    wait_pieces(piece_out, scan_send.at[1])
    wait_rows(gstate_buf, scan_send.at[2])
    wait_pieces(gpiece_out, scan_send.at[3])
    for copy in grad_in:
        copy.wait_send()
    qg_out.wait()
    kg_out.wait()
    vg_out.wait()
    own_att.wait()
    for copy in att_out:
        copy.wait()


def per_device(queries, key_vectors, value_vectors, out_grad):
    flat = jax.ShapeDtypeStruct((ROWS, D), BF)
    hbm = pl.BlockSpec(memory_space=pltpu.HBM)
    vm = pltpu.VMEM
    dma = pltpu.SemaphoreType.DMA
    att, qg, kg, vg = pl.pallas_call(
        kernel,
        out_shape=(jax.ShapeDtypeStruct((BLK, NHEAD, HL, D), BF), flat, flat, flat),
        in_specs=[hbm] * 4,
        out_specs=[hbm] * 4,
        scratch_shapes=[
            vm((ROWS, D), BF), vm((ROWS, D), BF), vm((ROWS, D), BF),
            vm((TOK, HL, D), BF), vm((ROWS, D), BF), vm((TOK, HL, D), BF),
            vm((ROWS, D), F32), vm((ROWS, D), F32), vm((ROWS, D), F32),
            vm((ROWS, D), BF), vm((ROWS, D), BF), vm((ROWS, D), BF),
            vm((NCH, D, HL * D), F32), vm((NCH, D, HL * D), F32),
            vm((NCH, HL * D, D), BF), vm((NCH, CH, CH), BF), vm((ROWS, D), F32),
            vm((CH, HL * D), BF), vm((CH, CH), BF), vm((CH, CH), BF),
            vm((D, HL * D), F32),
            vm((HL * D, D), F32), vm((NSEQ, PIECE, D), F32), vm((NSEQ, PIECE, D), BF), vm((HL * D, D), BF),
            vm((HL * D, D), F32), vm((NSEQ, PIECE, D), F32), vm((NSEQ, PIECE, D), BF), vm((HL * D, D), BF),
            dma((3,)), dma((3,)), dma((2 * NHEAD,)), dma((2 * NHEAD,)), dma((2,)), dma((4,)), dma((4,)),
        ],
        compiler_params=pltpu.CompilerParams(
            collective_id=0, has_side_effects=True, vmem_limit_bytes=56 * 2**20
        ),
        cost_estimate=pl.CostEstimate(flops=16 * 10**9, bytes_accessed=8 * 2**20, transcendentals=0),
        name="attend",
    )(
        queries.reshape(ROWS, D),
        key_vectors.reshape(ROWS, D),
        value_vectors.reshape(ROWS, D),
        out_grad.reshape(BLK, NHEAD, HL, D),
    )
    shape = (TOK, HL, D)
    return (att.reshape(BLK, NHEAD * HL, D), qg.reshape(shape), kg.reshape(shape), vg.reshape(shape))


def solution(mesh):
    return jax.shard_map(
        per_device,
        mesh=mesh,
        in_specs=(
            P("seq", "head", None),
            P("seq", "head", None),
            P("seq", "head", None),
            P(("seq", "head"), None, None),
        ),
        out_specs=(
            P(("seq", "head"), None, None),
            P("seq", "head", None),
            P("seq", "head", None),
            P("seq", "head", None),
        ),
        check_vma=False,
    )
```

time: 154 us -> 68 us (0.44)
  waiting for transfers between devices: 67.2 us -> 0 us
  Pallas kernels: 0 us -> 60.6 us
  matrix products: 28.8 us -> 0 us
  starting transfers between devices: 15.8 us -> 0 us
  between operations: 14.4 us -> 0.65 us
  other arithmetic: 10.8 us -> 0 us
  local copies, waits for them, and re-layouts: 16.7 us -> 6.53 us
    pallas_call x0 -> x1, Pallas kernels: none -> 60.6 us  [per_device(): pl.pallas_call(kernel, out_shape=(jax.ShapeDtypeStruct((BLK, NHEAD, HL, D...]
    all_gather x2 -> x0, waiting for transfers between devices: 38 us -> none  [the longest x1 34.7 us: per_device(): lax.all_gather(grad_state[None], 'seq', axis=0, tiled=True)]
    all_to_all x2 -> x0, waiting for transfers between devices: 29.1 us -> none  [the longest x1 29.1 us: per_device(): lax.all_to_all(out_grad, 'head', split_axis=1, concat_axis=0, tiled=True)]
    dot_general x20 -> x0, matrix products: 28.8 us -> none  [the longest x2 5.66 us: per_device(): jnp.einsum('hts,shd->thd', grad_scores, key_past, preferred_element_type=...]
    all_to_all x2 -> x0, starting transfers between devices: 15.7 us -> none  [the longest x1 9.01 us: per_device(): lax.all_to_all(out_grad, 'head', split_axis=1, concat_axis=0, tiled=True)]
    reduce_sum x2 -> x0, other arithmetic: 8.81 us -> none  [the longest x1 4.41 us: per_device(): prefix_sum = jnp.sum(below_mask * pieces[0], axis=0)]
    unnamed x41 -> x10, local copies, waits for them, and re-layouts: 10.6 us -> 6.53 us
    all_to_all x1 -> x0, local copies, waits for them, and re-layouts: 2.56 us -> none  [per_device(): lax.all_to_all(attended_heads, 'head', split_axis=0, concat_axis=1, tiled...]
  transfers between devices with their start and end apart: 4 -> 0, of which waited for: 3 -> 0; matrix products, arithmetic and copies ran while one was open for 31% -> 0% of each run, Pallas kernels for 0% -> 0%
where the time goes in v1:
time: 68 us; the launch traced here: 67.8 us
  Pallas kernels  60.6 us (89%)
  local copies, waits for them, and re-layouts  6.53 us (10%)
    pallas_call x1, Pallas kernels, per_device(): pl.pallas_call(kernel, out_shape=(jax.ShapeDtypeStruct((BLK, NHEAD, HL, D...  60.6 us
    unnamed x10, local copies, waits for them, and re-layouts  6.53 us

profile of v1, /device:TPU:1, one launch (start us, length us, event | category | flops | bytes accessed | tf_op | source)
XLA Modules:
  0.0 67.8 jit_solution(12936404622637567307)
XLA Ops:
  0.6 60.6 %attend.1 = (bf16[128,8,4,128]{3,2,1,0:T(4,128)(2,1)}, bf16[4096,128]{1,0:T(8,128)(2,1)}, bf16[4096,128]{1,0:T(8,128)(2,1)}, bf16[4096,128]{1,0:T(8,128)(2,1)}) custom-call(bf16[4096,128]{1,0:T(8,128)(2,1)} %bitcast.12, bf16[4096,128]{1,0:T(8,128)(2,1)} %bitcast.13, bf16[4096,128]{1,0:T(8,128)(2,1)} %bitcast.14, bf16[128,8,4,128]{3,2,1,0:T(4,128)(2,1)} %bitcast.15), custom_call_target="tpu_custom_call" | custom-call | flops 16000000000 | bytes 8388608 | tf_op jit(solution)/shard_map/attend/pallas_call | solution.py:298
  61.3 0.0 copy-start.2
  61.3 2.4 %copy.12 = bf16[128,32,128]{2,1,0:T(8,128)(2,1)} copy(bf16[128,32,128]{2,1,0:T(8,128)(2,1)} %bitcast.11) | data formatting | bytes 2097152
  63.6 0.0 copy-done.2
  63.6 0.0 copy-start.1
  63.6 1.0 %copy.13 = bf16[1024,4,128]{2,1,0:T(4,128)(2,1)} copy(bf16[1024,4,128]{2,1,0:T(4,128)(2,1)S(1)} %bitcast.10) | data formatting | bytes 2097152
  64.6 0.6 copy-done.1
  65.2 0.0 copy-start
  65.2 1.0 %copy.14 = bf16[1024,4,128]{2,1,0:T(4,128)(2,1)} copy(bf16[1024,4,128]{2,1,0:T(4,128)(2,1)S(1)} %bitcast.9) | data formatting | bytes 2097152
  66.2 0.6 copy-done
  66.8 1.0 %copy.15 = bf16[1024,4,128]{2,1,0:T(4,128)(2,1)} copy(bf16[1024,4,128]{2,1,0:T(4,128)(2,1)S(1)} %bitcast.8) | data formatting | bytes 2097152
Async XLA Ops:
  61.3 2.4 %copy-start.2 = (bf16[4096,128]{1,0:T(8,128)(2,1)S(1)}, bf16[4096,128]{1,0:T(8,128)(2,1)}, u32[]{:S(2)}) copy-start(bf16[4096,128]{1,0:T(8,128)(2,1)} %get-tuple-element.9) | copy-start | bytes 3145732
  63.6 1.6 %copy-start.1 = (bf16[4096,128]{1,0:T(8,128)(2,1)S(1)}, bf16[4096,128]{1,0:T(8,128)(2,1)}, u32[]{:S(2)}) copy-start(bf16[4096,128]{1,0:T(8,128)(2,1)} %get-tuple-element.10) | copy-start | bytes 3145732
  65.2 1.6 %copy-start = (bf16[4096,128]{1,0:T(8,128)(2,1)S(1)}, bf16[4096,128]{1,0:T(8,128)(2,1)}, u32[]{:S(2)}) copy-start(bf16[4096,128]{1,0:T(8,128)(2,1)} %get-tuple-element.11) | copy-start | bytes 3145732

commit v2 on v1

--- a/solution.py
+++ b/solution.py
@@ -18,6 +18,7 @@
 BLK = TOK // NHEAD
 CH = 256
 NCH = ROWS // CH
+BLOCK = BLK * HL
 PIECE = HL * D // NSEQ
 SEND_ORDER = (4, 3, 5, 2, 6, 1, 7)
 
@@ -36,14 +37,14 @@
 
 def kernel(
     q_hbm, k_hbm, v_hbm, g_hbm,
-    att_hbm, qg_hbm, kg_hbm, vg_hbm,
+    att_out_buf, qg_buf, kg_buf, vg_buf,
     q_buf, k_buf, v_buf, g_land, gs_buf, att_buf,
-    att_loc, kg_loc, vg_loc, qg_buf, kg_buf, vg_buf,
-    k_run, g_run, p_chunk, within_t, scale_buf,
+    att_loc, kg_loc, vg_loc,
+    k_run, within_t, scale_buf,
     head_mask, tri_mask, tri_mask_t,
     acc, state_buf, piece_in, piece_out, prefix_buf,
     gstate_buf, gpiece_in, gpiece_out, suffix_buf,
-    load_sem, out_sem, z_send, z_recv, own_sem, scan_send, scan_recv,
+    load_sem, z_send, z_recv, own_sem, scan_send, scan_recv,
 ):
     me = lax.axis_index("seq")
     z = lax.axis_index("head")
@@ -87,7 +88,8 @@
 
     row = lax.broadcasted_iota(jnp.int32, (CH, HL * D), 0)
     col = lax.broadcasted_iota(jnp.int32, (CH, HL * D), 1)
-    head_mask[...] = ((row & 3) == (col >> 7)).astype(F32).astype(BF)
+    for i in range(BLOCK // CH):
+        head_mask[i * CH : (i + 1) * CH] = ((row & 3) == (col >> 7)).astype(F32).astype(BF)
     row = lax.broadcasted_iota(jnp.int32, (CH, CH), 0)
     col = lax.broadcasted_iota(jnp.int32, (CH, CH), 1)
     same = (row & 3) == (col & 3)
@@ -98,7 +100,7 @@
         return pl.ds(pl.multiple_of(c * CH, CH), CH)
 
     def spread(x):
-        return jnp.concatenate([x] * HL, axis=1) * head_mask[...]
+        return jnp.concatenate([x] * HL, axis=1) * head_mask[: x.shape[0]]
 
     def wide(stacked):
         return jnp.concatenate([stacked[h * D : (h + 1) * D] for h in range(HL)], axis=1)
@@ -107,7 +109,7 @@
         return jnp.concatenate([w[:, h * D : (h + 1) * D] for h in range(HL)], axis=0)
 
     def each_chunk(body):
-        lax.fori_loop(0, NCH, lambda c, carry: (body(c), carry)[1], 0)
+        lax.fori_loop(0, NCH, lambda c, carry: (body(c), carry)[1], 0, unroll=4)
 
     def scatter_pieces(src, dst, k):
         def one(d, carry):
@@ -153,61 +155,75 @@
     loads[0].wait()
     loads[1].wait()
 
-    def key_state(c):
-        k_run[c] = acc[...]
-        acc[...] += tn(k_buf[rows(c)], spread(v_buf[rows(c)]))
-
-    each_chunk(key_state)
+    def key_total(i, carry):
+        part = pl.ds(pl.multiple_of(i * BLOCK, BLOCK), BLOCK)
+        acc[...] += tn(k_buf[part], spread(v_buf[part]))
+        return carry
+
+    lax.fori_loop(0, ROWS // BLOCK, key_total, 0)
     state_buf[...] = stack(acc[...])
     scatter_pieces(state_buf, piece_in, 0)
 
     loads[2].wait()
+    acc[...] = jnp.zeros_like(acc)
 
     def local_attend(c):
-        q, k = q_buf[rows(c)], k_buf[rows(c)]
+        q, k, v = q_buf[rows(c)], k_buf[rows(c)], v_buf[rows(c)]
+        before = stack(acc[...])
+        k_run[c] = before
+        acc[...] += tn(k, spread(v))
         within = nt(q, k).astype(BF) * tri_mask[...]
-        att_loc[rows(c)] = nn(within, v_buf[rows(c)])
+        att_loc[rows(c)] = nn(within, v) + nn(spread(q), before.astype(BF))
+
+    each_chunk(local_attend)
+
+    wait_pieces(piece_in, scan_recv.at[0])
+
+    def scan_up(j, run):
+        piece_out[j] = run.astype(BF)
+        return run + piece_in[j]
+
+    lax.fori_loop(0, NSEQ, scan_up, jnp.zeros((PIECE, D), F32))
+    return_pieces(piece_out, prefix_buf, 1)
+
+    def local_within_t(c):
+        within_t[c] = nt(k_buf[rows(c)], q_buf[rows(c)]).astype(BF) * tri_mask_t[...]
         token = lax.broadcasted_iota(jnp.int32, (CH, D), 0) >> 2
         position = (me * TOK + c * (CH // HL) + token).astype(F32)
         scale_buf[rows(c)] = 1.0 / jnp.sqrt(D * (position + 1.0))
 
-    each_chunk(local_attend)
-
-    wait_pieces(piece_in, scan_recv.at[0])
-
-    def scan_up(j, run):
-        piece_out[j] = run.astype(BF)
-        return run + piece_in[j]
-
-    lax.fori_loop(0, NSEQ, scan_up, jnp.zeros((PIECE, D), F32))
-    return_pieces(piece_out, prefix_buf, 1)
-
-    def local_within_t(c):
-        within_t[c] = nt(k_buf[rows(c)], q_buf[rows(c)]).astype(BF) * tri_mask_t[...]
-
     each_chunk(local_within_t)
     wait_rows(prefix_buf, scan_recv.at[1])
 
     att_rows = att_buf.reshape(ROWS, D)
 
     def attend(c):
-        prefix = (prefix_buf[...].astype(F32) + stack(k_run[c])).astype(BF)
-        p_chunk[c] = prefix
-        total = att_loc[rows(c)] + nn(spread(q_buf[rows(c)]), prefix)
+        total = att_loc[rows(c)] + nn(spread(q_buf[rows(c)]), prefix_buf[...])
         att_rows[rows(c)] = (scale_buf[rows(c)] * total).astype(BF)
 
     each_chunk(attend)
-
-    own_grad.wait()
-    for copy in grad_in:
-        copy.wait_recv()
+    own_att = pltpu.make_async_copy(
+        att_buf.at[pl.ds(z * BLK, BLK)], att_out_buf.at[:, z], own_sem.at[1]
+    )
+    own_att.start()
+
+    g_rows = g_land.reshape(ROWS, D)
+    acc[...] = jnp.zeros_like(acc)
+
+    def grad_block(source):
+        for half in range(BLOCK // CH):
+            part = pl.ds(pl.multiple_of(source * BLOCK + half * CH, CH), CH)
+            gs_buf[part] = (scale_buf[part] * g_rows[part].astype(F32)).astype(BF)
+        part = pl.ds(pl.multiple_of(source * BLOCK, BLOCK), BLOCK)
+        acc[...] += tn(q_buf[part], spread(gs_buf[part]))
 
     att_out = []
-    for d in SEND_ORDER:
+
+    def send_out(d):
         to = lax.rem(z + d, NHEAD)
         copy = pltpu.make_async_remote_copy(
             src_ref=att_buf.at[pl.ds(to * BLK, BLK)],
-            dst_ref=att_hbm.at[:, z],
+            dst_ref=att_out_buf.at[:, z],
             send_sem=z_send.at[NHEAD + d],
             recv_sem=z_recv.at[NHEAD + d],
             device_id={"head": to},
@@ -215,34 +231,28 @@
         )
         copy.start()
         att_out.append(copy)
-    own_att = pltpu.make_async_copy(
-        att_buf.at[pl.ds(z * BLK, BLK)], att_hbm.at[:, z], own_sem.at[1]
-    )
-    own_att.start()
-
-    g_rows = g_land.reshape(ROWS, D)
-    acc[...] = jnp.zeros_like(acc)
-
-    def grad_state(i):
-        c = NCH - 1 - i
-        g = (scale_buf[rows(c)] * g_rows[rows(c)].astype(F32)).astype(BF)
-        gs_buf[rows(c)] = g
-        g_run[c] = acc[...]
-        acc[...] += tn(q_buf[rows(c)], spread(g))
-
-    each_chunk(grad_state)
+
+    for d in SEND_ORDER[:2]:
+        send_out(d)
+    own_grad.wait()
+    grad_block(z)
+    for i, d in enumerate(SEND_ORDER):
+        grad_in[i].wait_recv()
+        for e in SEND_ORDER[i + 2 : i + 2 + 1]:
+            send_out(e)
+        grad_block(lax.rem(z + NHEAD - d, NHEAD))
+
     gstate_buf[...] = stack(acc[...])
     scatter_pieces(gstate_buf, gpiece_in, 2)
 
     def query_grad(c):
         g = gs_buf[rows(c)]
+        prefix = (prefix_buf[...].astype(F32) + k_run[c]).astype(BF)
         scores = nt(g, v_buf[rows(c)]).astype(BF) * tri_mask[...]
-        total = nt(spread(g), wide(p_chunk[c])) + nn(scores, k_buf[rows(c)])
+        total = nt(spread(g), wide(prefix)) + nn(scores, k_buf[rows(c)])
         qg_buf[rows(c)] = total.astype(BF)
 
     each_chunk(query_grad)
-    qg_out = pltpu.make_async_copy(qg_buf, qg_hbm, out_sem.at[0])
-    qg_out.start()
 
     wait_pieces(gpiece_in, scan_recv.at[2])
 
@@ -254,27 +264,28 @@
     lax.fori_loop(0, NSEQ, scan_down, jnp.zeros((PIECE, D), F32))
     return_pieces(gpiece_out, suffix_buf, 3)
 
-    def local_key_value(c):
-        g = gs_buf[rows(c)]
+    acc[...] = jnp.zeros_like(acc)
+
+    def local_key_value(i):
+        c = NCH - 1 - i
+        g, q = gs_buf[rows(c)], q_buf[rows(c)]
+        after = acc[...].astype(BF)
+        acc[...] += tn(q, spread(g))
         scores_t = nt(v_buf[rows(c)], g).astype(BF) * tri_mask_t[...]
-        kg_loc[rows(c)] = nn(scores_t, q_buf[rows(c)])
-        vg_loc[rows(c)] = nn(within_t[c], g)
+        kg_loc[rows(c)] = nn(scores_t, q) + nt(spread(v_buf[rows(c)]), after)
+        vg_loc[rows(c)] = nn(within_t[c], g) + nn(spread(k_buf[rows(c)]), stack(after))
 
     each_chunk(local_key_value)
     wait_rows(suffix_buf, scan_recv.at[3])
 
     def key_value(c):
-        suffix = (suffix_buf[...].astype(F32) + stack(g_run[c])).astype(BF)
+        suffix = suffix_buf[...]
         kg = kg_loc[rows(c)] + nt(spread(v_buf[rows(c)]), wide(suffix))
         kg_buf[rows(c)] = kg.astype(BF)
         vg = vg_loc[rows(c)] + nn(spread(k_buf[rows(c)]), suffix)
         vg_buf[rows(c)] = vg.astype(BF)
 
     each_chunk(key_value)
-    kg_out = pltpu.make_async_copy(kg_buf, kg_hbm, out_sem.at[1])
-    kg_out.start()
-    vg_out = pltpu.make_async_copy(vg_buf, vg_hbm, out_sem.at[2])
-    vg_out.start()
 
     wait_rows(state_buf, scan_send.at[0])
     wait_pieces(piece_out, scan_send.at[1])
@@ -282,36 +293,40 @@
     wait_pieces(gpiece_out, scan_send.at[3])
     for copy in grad_in:
         copy.wait_send()
-    qg_out.wait()
-    kg_out.wait()
-    vg_out.wait()
     own_att.wait()
     for copy in att_out:
         copy.wait()
 
 
+def store_kernel(*refs):
+    sources, targets, sem = refs[:4], refs[4:8], refs[8]
+    copies = [pltpu.make_async_copy(sources[i], targets[i], sem.at[i]) for i in range(4)]
+    for copy in copies:
+        copy.start()
+    for copy in copies:
+        copy.wait()
+
+
 def per_device(queries, key_vectors, value_vectors, out_grad):
-    flat = jax.ShapeDtypeStruct((ROWS, D), BF)
     hbm = pl.BlockSpec(memory_space=pltpu.HBM)
     vm = pltpu.VMEM
+    in_vmem = pl.BlockSpec(memory_space=vm)
     dma = pltpu.SemaphoreType.DMA
-    att, qg, kg, vg = pl.pallas_call(
+    held = pl.pallas_call(
         kernel,
-        out_shape=(jax.ShapeDtypeStruct((BLK, NHEAD, HL, D), BF), flat, flat, flat),
+        out_shape=(vm((BLK, NHEAD, HL, D), BF), vm((ROWS, D), BF), vm((ROWS, D), BF), vm((ROWS, D), BF)),
         in_specs=[hbm] * 4,
-        out_specs=[hbm] * 4,
+        out_specs=[in_vmem] * 4,
         scratch_shapes=[
             vm((ROWS, D), BF), vm((ROWS, D), BF), vm((ROWS, D), BF),
             vm((TOK, HL, D), BF), vm((ROWS, D), BF), vm((TOK, HL, D), BF),
             vm((ROWS, D), F32), vm((ROWS, D), F32), vm((ROWS, D), F32),
-            vm((ROWS, D), BF), vm((ROWS, D), BF), vm((ROWS, D), BF),
-            vm((NCH, D, HL * D), F32), vm((NCH, D, HL * D), F32),
-            vm((NCH, HL * D, D), BF), vm((NCH, CH, CH), BF), vm((ROWS, D), F32),
-            vm((CH, HL * D), BF), vm((CH, CH), BF), vm((CH, CH), BF),
+            vm((NCH, HL * D, D), F32), vm((NCH, CH, CH), BF), vm((ROWS, D), F32),
+            vm((BLOCK, HL * D), BF), vm((CH, CH), BF), vm((CH, CH), BF),
             vm((D, HL * D), F32),
             vm((HL * D, D), F32), vm((NSEQ, PIECE, D), F32), vm((NSEQ, PIECE, D), BF), vm((HL * D, D), BF),
             vm((HL * D, D), F32), vm((NSEQ, PIECE, D), F32), vm((NSEQ, PIECE, D), BF), vm((HL * D, D), BF),
-            dma((3,)), dma((3,)), dma((2 * NHEAD,)), dma((2 * NHEAD,)), dma((2,)), dma((4,)), dma((4,)),
+            dma((3,)), dma((2 * NHEAD,)), dma((2 * NHEAD,)), dma((2,)), dma((4,)), dma((4,)),
         ],
         compiler_params=pltpu.CompilerParams(
             collective_id=0, has_side_effects=True, vmem_limit_bytes=56 * 2**20
@@ -324,6 +339,15 @@
         value_vectors.reshape(ROWS, D),
         out_grad.reshape(BLK, NHEAD, HL, D),
     )
+    att, qg, kg, vg = pl.pallas_call(
+        store_kernel,
+        out_shape=[jax.ShapeDtypeStruct(x.shape, x.dtype) for x in held],
+        in_specs=[pl.BlockSpec(memory_space=pl.ANY)] * 4,
+        out_specs=[hbm] * 4,
+        scratch_shapes=[dma((4,))],
+        compiler_params=pltpu.CompilerParams(vmem_limit_bytes=2**20),
+        name="store",
+    )(*held)
     shape = (TOK, HL, D)
     return (att.reshape(BLK, NHEAD * HL, D), qg.reshape(shape), kg.reshape(shape), vg.reshape(shape))
 

time: 68 us -> 61.9 us (0.910)
  local copies, waits for them, and re-layouts: 6.53 us -> 0 us
    unnamed x10 -> x0, local copies, waits for them, and re-layouts: 6.53 us -> none
    pallas_call x1 -> x2, Pallas kernels: 60.6 us -> 61.2 us  [the longest x1 59.1 us: per_device(): pl.pallas_call(kernel, out_shape=(vm((BLK, NHEAD, HL, D), BF), vm((ROWS,...]
where the time goes in v2:
time: 61.9 us; the launch traced here: 61.8 us
  Pallas kernels  61.2 us (99%)
  between operations  0.64 us (1%)
    pallas_call x1, Pallas kernels, per_device(): pl.pallas_call(kernel, out_shape=(vm((BLK, NHEAD, HL, D), BF), vm((ROWS,...  59.1 us
    pallas_call x1, Pallas kernels, per_device(): pl.pallas_call(store_kernel, out_shape=[jax.ShapeDtypeStruct(x.shape, x.d...  2.04 us

profile of v2, /device:TPU:1, one launch (start us, length us, event | category | flops | bytes accessed | tf_op | source)
XLA Modules:
  0.0 61.8 jit_solution(17186263795789678482)
XLA Ops:
  0.6 59.1 %attend.1 = (bf16[128,8,4,128]{3,2,1,0:T(4,128)(2,1)S(1)}, bf16[4096,128]{1,0:T(8,128)(2,1)S(1)}, bf16[4096,128]{1,0:T(8,128)(2,1)S(1)}, bf16[4096,128]{1,0:T(8,128)(2,1)S(1)}) custom-call(bf16[4096,128]{1,0:T(8,128)(2,1)} %bitcast.8, bf16[4096,128]{1,0:T(8,128)(2,1)} %bitcast.9, bf16[4096,128]{1,0:T(8,128)(2,1)} %bitcast.10, bf16[128,8,4,128]{3,2,1,0:T(4,128)(2,1)} %bitcast.11), custom_call_target="tpu_custom_call" | custom-call | flops 16000000000 | bytes 8388608 | tf_op jit(solution)/shard_map/attend/pallas_call | solution.py:315
  59.8 2.0 %store.1 = (bf16[128,8,4,128]{3,2,1,0:T(4,128)(2,1)}, bf16[4096,128]{1,0:T(8,128)(2,1)}, bf16[4096,128]{1,0:T(8,128)(2,1)}, bf16[4096,128]{1,0:T(8,128)(2,1)}) custom-call(bf16[128,8,4,128]{3,2,1,0:T(4,128)(2,1)S(1)} %get-tuple-element.12.refs_0_, bf16[4096,128]{1,0:T(8,128)(2,1)S(1)} %get-tuple-element.13.refs_1_, ...), custom_call_target="tpu_custom_call" | custom-call | tf_op jit(solution)/shard_map/store/pallas_call | solution.py:342

commit v3 on v2

--- a/solution.py
+++ b/solution.py
@@ -20,6 +20,7 @@
 NCH = ROWS // CH
 BLOCK = BLK * HL
 PIECE = HL * D // NSEQ
+GATE = 3
 SEND_ORDER = (4, 3, 5, 2, 6, 1, 7)
 
 
@@ -44,7 +45,7 @@
     head_mask, tri_mask, tri_mask_t,
     acc, state_buf, piece_in, piece_out, prefix_buf,
     gstate_buf, gpiece_in, gpiece_out, suffix_buf,
-    load_sem, z_send, z_recv, own_sem, scan_send, scan_recv,
+    load_sem, z_send, z_recv, own_sem, scan_send, scan_recv, column_in, all_in,
 ):
     me = lax.axis_index("seq")
     z = lax.axis_index("head")
@@ -57,18 +58,23 @@
 
     barrier = pltpu.get_barrier_semaphore()
     for d in range(1, NHEAD):
-        pl.semaphore_signal(
-            barrier, inc=1, device_id={"head": lax.rem(z + d, NHEAD)}, device_id_type=MESH
-        )
-
-    def greet(d, carry):
-        pl.semaphore_signal(
-            barrier, inc=1, device_id={"seq": lax.rem(me + d, NSEQ)}, device_id_type=MESH
-        )
-        return carry
-
-    lax.fori_loop(1, NSEQ, greet, 0)
-    pl.semaphore_wait(barrier, NHEAD - 1 + NSEQ - 1)
+        to = lax.rem(z + d, NHEAD)
+
+        @pl.when(to != GATE)
+        def _():
+            pl.semaphore_signal(barrier, inc=1, device_id={"head": to}, device_id_type=MESH)
+
+    @pl.when(z != GATE)
+    def _():
+        pl.semaphore_wait(barrier, NHEAD - 1)
+
+    @pl.when(z == GATE + 1)
+    def _():
+        pl.semaphore_signal(column_in, inc=1, device_id={"head": GATE}, device_id_type=MESH)
+
+    @pl.when(z == GATE)
+    def _():
+        pl.semaphore_wait(column_in, 1)
 
     grad_in = []
     for d in SEND_ORDER:
@@ -86,6 +92,16 @@
     own_grad = pltpu.make_async_copy(g_hbm.at[:, z], g_land.at[pl.ds(z * BLK, BLK)], own_sem.at[0])
     own_grad.start()
 
+    @pl.when(z == GATE)
+    def _():
+        def greet(d, carry):
+            pl.semaphore_signal(
+                barrier, inc=1, device_id={"seq": lax.rem(me + d, NSEQ)}, device_id_type=MESH
+            )
+            return carry
+
+        lax.fori_loop(1, NSEQ, greet, 0)
+
     row = lax.broadcasted_iota(jnp.int32, (CH, HL * D), 0)
     col = lax.broadcasted_iota(jnp.int32, (CH, HL * D), 1)
     for i in range(BLOCK // CH):
@@ -108,8 +124,8 @@
     def stack(w):
         return jnp.concatenate([w[:, h * D : (h + 1) * D] for h in range(HL)], axis=0)
 
-    def each_chunk(body):
-        lax.fori_loop(0, NCH, lambda c, carry: (body(c), carry)[1], 0, unroll=4)
+    def each_chunk(body, unroll=4):
+        lax.fori_loop(0, NCH, lambda c, carry: (body(c), carry)[1], 0, unroll=unroll)
 
     def scatter_pieces(src, dst, k):
         def one(d, carry):
@@ -162,6 +178,19 @@
 
     lax.fori_loop(0, ROWS // BLOCK, key_total, 0)
     state_buf[...] = stack(acc[...])
+
+    @pl.when(z == GATE)
+    def _():
+        pl.semaphore_wait(barrier, NSEQ - 1)
+        for d in range(1, NHEAD):
+            pl.semaphore_signal(
+                all_in, inc=1, device_id={"head": lax.rem(z + d, NHEAD)}, device_id_type=MESH
+            )
+
+    @pl.when(z != GATE)
+    def _():
+        pl.semaphore_wait(all_in, 1)
+
     scatter_pieces(state_buf, piece_in, 0)
 
     loads[2].wait()
@@ -252,7 +281,7 @@
         total = nt(spread(g), wide(prefix)) + nn(scores, k_buf[rows(c)])
         qg_buf[rows(c)] = total.astype(BF)
 
-    each_chunk(query_grad)
+    each_chunk(query_grad, 8)
 
     wait_pieces(gpiece_in, scan_recv.at[2])
 
@@ -275,7 +304,7 @@
         kg_loc[rows(c)] = nn(scores_t, q) + nt(spread(v_buf[rows(c)]), after)
         vg_loc[rows(c)] = nn(within_t[c], g) + nn(spread(k_buf[rows(c)]), stack(after))
 
-    each_chunk(local_key_value)
+    each_chunk(local_key_value, 8)
     wait_rows(suffix_buf, scan_recv.at[3])
 
     def key_value(c):
@@ -285,7 +314,7 @@
         vg = vg_loc[rows(c)] + nn(spread(k_buf[rows(c)]), suffix)
         vg_buf[rows(c)] = vg.astype(BF)
 
-    each_chunk(key_value)
+    each_chunk(key_value, 8)
 
     wait_rows(state_buf, scan_send.at[0])
     wait_pieces(piece_out, scan_send.at[1])
@@ -327,6 +356,7 @@
             vm((HL * D, D), F32), vm((NSEQ, PIECE, D), F32), vm((NSEQ, PIECE, D), BF), vm((HL * D, D), BF),
             vm((HL * D, D), F32), vm((NSEQ, PIECE, D), F32), vm((NSEQ, PIECE, D), BF), vm((HL * D, D), BF),
             dma((3,)), dma((2 * NHEAD,)), dma((2 * NHEAD,)), dma((2,)), dma((4,)), dma((4,)),
+            pltpu.SemaphoreType.REGULAR, pltpu.SemaphoreType.REGULAR,
         ],
         compiler_params=pltpu.CompilerParams(
             collective_id=0, has_side_effects=True, vmem_limit_bytes=56 * 2**20

time: 61.9 us -> 58.9 us (0.952)
  Pallas kernels: 61.2 us -> 58.2 us
    pallas_call x1, Pallas kernels: 59.1 us -> 56.2 us  [per_device(): pl.pallas_call(kernel, out_shape=(vm((BLK, NHEAD, HL, D), BF), vm((ROWS,...]
where the time goes in v3:
time: 58.9 us
  Pallas kernels  58.2 us (99%)
  between operations  0.64 us (1%)
    pallas_call x1, Pallas kernels, per_device(): pl.pallas_call(kernel, out_shape=(vm((BLK, NHEAD, HL, D), BF), vm((ROWS,...  56.2 us
    pallas_call x1, Pallas kernels, per_device(): pl.pallas_call(store_kernel, out_shape=[jax.ShapeDtypeStruct(x.shape, x.d...  2.04 us

profile of v3, /device:TPU:1, one launch (start us, length us, event | category | flops | bytes accessed | tf_op | source)
XLA Modules:
  0.0 58.9 jit_solution(16621417961797121618)
XLA Ops:
  0.6 56.2 %attend.1 = (bf16[128,8,4,128]{3,2,1,0:T(4,128)(2,1)S(1)}, bf16[4096,128]{1,0:T(8,128)(2,1)S(1)}, bf16[4096,128]{1,0:T(8,128)(2,1)S(1)}, bf16[4096,128]{1,0:T(8,128)(2,1)S(1)}) custom-call(bf16[4096,128]{1,0:T(8,128)(2,1)} %bitcast.8, bf16[4096,128]{1,0:T(8,128)(2,1)} %bitcast.9, bf16[4096,128]{1,0:T(8,128)(2,1)} %bitcast.10, bf16[128,8,4,128]{3,2,1,0:T(4,128)(2,1)} %bitcast.11), custom_call_target="tpu_custom_call" | custom-call | flops 16000000000 | bytes 8388608 | tf_op jit(solution)/shard_map/attend/pallas_call | solution.py:344
  56.8 2.0 %store.1 = (bf16[128,8,4,128]{3,2,1,0:T(4,128)(2,1)}, bf16[4096,128]{1,0:T(8,128)(2,1)}, bf16[4096,128]{1,0:T(8,128)(2,1)}, bf16[4096,128]{1,0:T(8,128)(2,1)}) custom-call(bf16[128,8,4,128]{3,2,1,0:T(4,128)(2,1)S(1)} %get-tuple-element.12.refs_0_, bf16[4096,128]{1,0:T(8,128)(2,1)S(1)} %get-tuple-element.13.refs_1_, ...), custom_call_target="tpu_custom_call" | custom-call | tf_op jit(solution)/shard_map/store/pallas_call | solution.py:372

commit v4 on v3

--- a/solution.py
+++ b/solution.py
@@ -21,6 +21,7 @@
 BLOCK = BLK * HL
 PIECE = HL * D // NSEQ
 GATE = 3
+HOLD = 4
 SEND_ORDER = (4, 3, 5, 2, 6, 1, 7)
 
 
@@ -261,12 +262,15 @@
         copy.start()
         att_out.append(copy)
 
+    for copy in grad_in[:HOLD]:
+        copy.wait_recv()
     for d in SEND_ORDER[:2]:
         send_out(d)
     own_grad.wait()
     grad_block(z)
     for i, d in enumerate(SEND_ORDER):
-        grad_in[i].wait_recv()
+        if i >= HOLD:
+            grad_in[i].wait_recv()
         for e in SEND_ORDER[i + 2 : i + 2 + 1]:
             send_out(e)
         grad_block(lax.rem(z + NHEAD - d, NHEAD))

time: 58.9 us -> 59.2 us (level)
  no operation moved by 1% of the time
where the time goes in v4:
time: 59.2 us; the launch traced here: 58.9 us
  Pallas kernels  58.2 us (98%)
  between operations  0.64 us (1%)
    pallas_call x1, Pallas kernels, per_device(): pl.pallas_call(kernel, out_shape=(vm((BLK, NHEAD, HL, D), BF), vm((ROWS,...  56.2 us
    pallas_call x1, Pallas kernels, per_device(): pl.pallas_call(store_kernel, out_shape=[jax.ShapeDtypeStruct(x.shape, x.d...  2.04 us

profile of v4, /device:TPU:1, one launch (start us, length us, event | category | flops | bytes accessed | tf_op | source)
XLA Modules:
  0.0 58.9 jit_solution(5313667447727374370)
XLA Ops:
  0.6 56.2 %attend.1 = (bf16[128,8,4,128]{3,2,1,0:T(4,128)(2,1)S(1)}, bf16[4096,128]{1,0:T(8,128)(2,1)S(1)}, bf16[4096,128]{1,0:T(8,128)(2,1)S(1)}, bf16[4096,128]{1,0:T(8,128)(2,1)S(1)}) custom-call(bf16[4096,128]{1,0:T(8,128)(2,1)} %bitcast.8, bf16[4096,128]{1,0:T(8,128)(2,1)} %bitcast.9, bf16[4096,128]{1,0:T(8,128)(2,1)} %bitcast.10, bf16[128,8,4,128]{3,2,1,0:T(4,128)(2,1)} %bitcast.11), custom_call_target="tpu_custom_call" | custom-call | flops 16000000000 | bytes 8388608 | tf_op jit(solution)/shard_map/attend/pallas_call | solution.py:348
  56.8 2.0 %store.1 = (bf16[128,8,4,128]{3,2,1,0:T(4,128)(2,1)}, bf16[4096,128]{1,0:T(8,128)(2,1)}, bf16[4096,128]{1,0:T(8,128)(2,1)}, bf16[4096,128]{1,0:T(8,128)(2,1)}) custom-call(bf16[128,8,4,128]{3,2,1,0:T(4,128)(2,1)S(1)} %get-tuple-element.12.refs_0_, bf16[4096,128]{1,0:T(8,128)(2,1)S(1)} %get-tuple-element.13.refs_1_, ...), custom_call_target="tpu_custom_call" | custom-call | tf_op jit(solution)/shard_map/store/pallas_call | solution.py:376
